TPU v7x, 512 devices: a whole 4x8x8 slice. The times are simulated.
512 devices in a mesh: clips: 4 (over x), tm: 8 (over y), tile: 16 (over z, core).
Axes of the slice: x: 4, y: 8, z: 8, core: 2. Of those that a mesh axis runs over, the one named last changes fastest.
Arguments:
- video: bfloat16 [4, 32, 96, 64, 256], P('clips', 'tm', None, 'tile')
- norm1_gain: float32 [96], replicated, may hold values from 0.1 to 1.9
- conv1_weight: bfloat16 [3, 3, 3, 96, 96], replicated, may hold values from -0.21875 to 0.21875
- conv1_bias: float32 [96], replicated, may hold values from -3 to 3
- norm2_gain: float32 [96], replicated, may hold values from 0.1 to 1.9
- conv2_weight: bfloat16 [3, 3, 3, 96, 96], replicated, may hold values from -0.21875 to 0.21875
- conv2_bias: float32 [96], replicated, may hold values from -3 to 3
- down_weight: bfloat16 [3, 3, 96, 96], replicated, may hold values from -0.21875 to 0.21875
- down_bias: float32 [96], replicated, may hold values from -3 to 3
- proj_weight: bfloat16 [192, 96], replicated, may hold values from -0.625 to 0.625
- proj_bias: float32 [192], replicated, may hold values from -3 to 3
- dest_group: int32 [4, 32], replicated, may hold values from -1 to 3, as said below
- dest_slot: int32 [4, 32], replicated, may hold values from -1 to 3, as said below
Outputs:
- packed: bfloat16 [4, 8, 4, 192, 32, 128], P('clips', 'tm', None, None, 'tile')
Inputs may be any that keep to these rules, and one draw needn't show every extreme that they name: `dest_group`: -1 marks the frames past their clip's end; each clip's live frames are its first ones, at least (100) // 5 of them, and one clip has all 32. A frame stays at its span index f // 4. From one span of one clip at most 2 frames go to any one group, and some span sends that many. `dest_slot`: -1 exactly where dest_group is -1. Frames that go to one group from one span index, over all clips, have distinct positions; some group receives 4 frames at some span index.
All inputs are finite; a program needn't handle non-finite values.
Results may differ from a plain program's by a relative error of at most 0.014.
Values may be sent and summed in bfloat16 or wider, within the bound.
A program may use at most 64 MiB of HBM per device.

v0:
```python
import functools

import jax
import jax.numpy as jnp
from jax import lax
from jax.experimental import pallas as pl
from jax.experimental.pallas import tpu as pltpu
from jax.sharding import PartitionSpec as P

MESH = pl.DeviceIdType.MESH
EPS = 1e-06
C, C2, H, W, HALF = 96, 192, 4, 256, 128
BF, F32 = jnp.bfloat16, jnp.float32


def dot(a, b):
    return jnp.dot(a, b, preferred_element_type=F32)


def kernel(
    sizes,
    dgh, dsh, video, g1h, b1h, g2h, b2h, bdh, bph, w1h, w2h, dh, ph,
    out,
    vraw, vh, vht, vt, vn, a1, a2, s_out, s_in, bl, red, p_out, p_in, sel, got,
    w1raw, w2raw, draw, pw, w1f, w1m, w1e, w2f, w2m, w2l, w2e, w2p, dw,
    perm, rows, prow, cols, pcol, dg, ds, lsem, ssem, rsem,
):
    n_clips, n_tm, n_tile = sizes
    g = lax.axis_index("clips")
    t = lax.axis_index("tm")
    k = lax.axis_index("tile")
    up = {"tile": lax.rem(k + n_tile - 1, n_tile)}
    down = {"tile": lax.rem(k + 1, n_tile)}
    later = {"tm": lax.rem(t + 1, n_tm)}
    before = {"tm": lax.rem(t + n_tm - 1, n_tm)}
    others = [{"clips": lax.rem(g + 1 + j, n_clips)} for j in range(n_clips - 1)]
    first_span = t == 0
    top = k == 0
    bottom = k == n_tile - 1

    copies = {}

    def send(name, src, dst, device):
        i = len(copies)
        copy = pltpu.make_async_remote_copy(
            src_ref=src, dst_ref=dst, send_sem=ssem.at[i], recv_sem=rsem.at[i],
            device_id=device, device_id_type=MESH,
        )
        copy.start()
        copies[name] = copy

    def arrived(name):
        copies[name].wait_recv()

    locals_ = {}

    def fetch(name, src, dst):
        copy = pltpu.make_async_copy(src, dst, lsem.at[len(locals_)])
        copy.start()
        locals_[name] = copy

    barrier = pltpu.get_barrier_semaphore()
    peers = [up, down, later, before] + others
    for peer in peers:
        pl.semaphore_signal(barrier, inc=1, device_id=peer, device_id_type=MESH)
    for f in (2, 3, 1, 0):
        fetch(("v", f), video.at[f], vraw.at[f])
    for i, vector in enumerate((g1h, b1h, g2h, b2h, bdh)):
        fetch(("row", i), vector, rows.at[i])
    fetch("prow", bph, prow)
    fetch("w1", w1h, w1raw)
    fetch("w2", w2h, w2raw)
    fetch("d", dh, draw)
    fetch("p", ph, pw)
    fetch("dg", dgh, dg)
    fetch("ds", dsh, ds)

    src_col = lax.broadcasted_iota(jnp.int32, (W, W), 0)
    dst_col = lax.broadcasted_iota(jnp.int32, (W, W), 1)
    want = jnp.where(dst_col < HALF, 2 * dst_col, 2 * dst_col - (W - 1))
    perm[...] = (src_col == want).astype(F32).astype(BF)

    def column(row):
        n = row.shape[1]
        eye = lax.broadcasted_iota(jnp.int32, (n, n), 0) == lax.broadcasted_iota(jnp.int32, (n, n), 1)
        col = jnp.sum(jnp.where(eye, row, 0.0), axis=1, keepdims=True)
        return jnp.broadcast_to(col, (n, HALF))

    for i in range(5):
        locals_[("row", i)].wait()
        cols[i] = column(rows[i])
    locals_["prow"].wait()
    pcol[...] = column(prow[...])

    lane = lax.broadcasted_iota(jnp.int32, (C, HALF), 1)

    def halves(x):
        return x[:, :HALF], x[:, HALF:]

    def norm_silu(x, gain):
        ms = jnp.sum(x * x, axis=0, keepdims=True) * (1.0 / C)
        n = x * (lax.rsqrt(ms + EPS) * 0.5) * gain
        return n + n * jnp.tanh(n)

    def conv_row(a, frames, w, r):
        x = jnp.concatenate([a[f, pl.ds(r, 3)].reshape(3 * C, W) for f in frames], axis=0)
        y = dot(w[...], x)
        y0e, y0o = halves(y[:C])
        y1e, y1o = halves(y[C : 2 * C])
        y2e, y2o = halves(y[2 * C :])
        even = y1e + y2o + jnp.where(lane == 0, 0.0, pltpu.roll(y0o, 1, 1))
        odd = y1o + y0e + jnp.where(lane == HALF - 1, 0.0, pltpu.roll(y2e, HALF - 1, 1))
        return even, odd

    def turn(raw, dst):
        v = jnp.swapaxes(raw, 0, 1).reshape(H * C, W)
        dst[...] = dot(v, perm[...]).astype(BF).reshape(H, C, W)

    def first_act(src, index, keep=None):
        gain = cols[0]
        for r in range(H):
            for side in range(2):
                s = pl.ds(HALF * side, HALF)
                x = norm_silu(src[r, :, s].astype(F32), gain)
                if keep is not None:
                    x = jnp.where(keep, x, 0.0)
                a1[index, r + 1, :, s] = x.astype(BF)

    def send_a1(i):
        send(("a1up", i), a1.at[i, 1], a1.at[i, 5], up)
        send(("a1down", i), a1.at[i, 4], a1.at[i, 0], down)

    def take_a1(i):
        arrived(("a1up", i))
        arrived(("a1down", i))

        @pl.when(top)
        def _():
            a1[i, 0] = jnp.zeros((C, W), BF)

        @pl.when(bottom)
        def _():
            a1[i, 5] = jnp.zeros((C, W), BF)

    def send_a2(f):
        send(("a2up", f), a2.at[f, pl.ds(1, 2)], a2.at[f, pl.ds(5, 2)], up)
        send(("a2down", f), a2.at[f, 4], a2.at[f, 0], down)

    def take_a2(f):
        arrived(("a2up", f))
        arrived(("a2down", f))

        @pl.when(top)
        def _():
            a2[f, 0] = jnp.zeros((C, W), BF)

        @pl.when(bottom)
        def _():
            a2[f, pl.ds(5, 2)] = jnp.zeros((2, C, W), BF)

    def second_act(f, r, even, odd):
        for side, x in enumerate((even, odd)):
            x = (x + cols[1]).astype(BF).astype(F32)
            a2[f, r + 1, :, pl.ds(HALF * side, HALF)] = norm_silu(x, cols[2]).astype(BF)

    pl.semaphore_wait(barrier, len(peers))
    send("v", video.at[3], vh, later)

    for f in (2, 3, 1, 0):
        locals_[("v", f)].wait()
        turn(vraw[f], vt.at[f])
        first_act(vt.at[f], f + 1)
        send_a1(f + 1)
        send(("vt", f), vt.at[f, 0], vn.at[f], up)

    def gather_taps(raw, taps):
        return jnp.concatenate([raw[3 * i + j] for i in taps for j in range(3)], axis=1)

    locals_["w1"].wait()
    w1e[...] = gather_taps(w1raw, (0,))
    take_a1(3)
    for r in range(H):
        even, odd = conv_row(a1, (3,), w1e, r)
        s_out[r, :, pl.ds(0, HALF)] = even.astype(BF)
        s_out[r, :, pl.ds(HALF, HALF)] = odd.astype(BF)
    send("s", s_out, s_in, later)

    w1f[...] = gather_taps(w1raw, (0, 1, 2))
    w1m[...] = gather_taps(w1raw, (1, 2))
    take_a1(4)
    take_a1(2)
    for r in range(H):
        second_act(3, r, *conv_row(a1, (2, 3, 4), w1f, r))
    send_a2(3)
    take_a1(1)
    for r in range(H):
        second_act(2, r, *conv_row(a1, (1, 2, 3), w1f, r))
    send_a2(2)

    locals_["w2"].wait()
    w2f[...] = gather_taps(w2raw, (0, 1, 2))
    w2p[...] = gather_taps(w2raw, (0, 1))
    w2m[...] = gather_taps(w2raw, (1, 2))
    w2e[...] = gather_taps(w2raw, (0,))
    w2l[...] = gather_taps(w2raw, (2,))
    locals_["d"].wait()
    dw[...] = jnp.concatenate([draw[i] for i in range(9)], axis=1)

    def block_row(slot, r, even, odd):
        if r == H:
            even = jnp.where(bottom, 0.0, even)
            odd = jnp.where(bottom, 0.0, odd)
        even = even.astype(BF).astype(F32)
        bl[slot, r, 0] = even.astype(BF)
        bl[slot, r, 1] = odd.astype(BF)
        bl[slot, r, 2] = jnp.where(lane == HALF - 1, 0.0, pltpu.roll(even, HALF - 1, 1)).astype(BF)

    def shrink(slot):
        x = jnp.concatenate([bl[slot, pl.ds(2 * q, 3)].reshape(9 * C, HALF) for q in range(2)], axis=1)
        return dot(dw[...], x)

    take_a2(3)
    take_a2(2)
    for r in range(H + 1):
        block_row(0, r, *conv_row(a2, (2, 3), w2p, r))
        block_row(1, r, *conv_row(a2, (3,), w2e, r))
    for i in range(2):
        p_out[i] = shrink(i).astype(BF)
    send("p", p_out, p_in, later)

    arrived("v")
    turn(vh[...], vht)
    first_act(vht, 0, jnp.logical_not(first_span))
    send_a1(0)
    take_a1(0)
    for r in range(H):
        second_act(1, r, *conv_row(a1, (0, 1, 2), w1f, r))
    send_a2(1)
    arrived("s")
    for r in range(H):
        even, odd = conv_row(a1, (0, 1), w1m, r)
        se, so = halves(jnp.where(first_span, 0.0, s_in[r].astype(F32)))
        second_act(0, r, even + se, odd + so)
    send_a2(0)

    for f in range(H):
        arrived(("vt", f))

    def block_frame(f, frames, w):
        for r in range(H + 1):
            even, odd = conv_row(a2, frames, w, r)
            ve, vo = halves((vt[f, r] if r < H else vn[f]).astype(F32))
            block_row(f, r, even + cols[3] + ve, odd + cols[3] + vo)

    bias = jnp.concatenate([cols[4], cols[4]], axis=1)
    take_a2(1)
    block_frame(3, (1, 2, 3), w2f)
    red[3] = (shrink(3) + bias).astype(BF)
    take_a2(0)
    block_frame(2, (0, 1, 2), w2f)
    red[2] = (shrink(2) + bias).astype(BF)
    block_frame(1, (0, 1), w2m)
    block_frame(0, (0,), w2l)
    arrived("p")
    for f in range(2):
        part = jnp.where(first_span, 0.0, p_in[f].astype(F32))
        red[f] = (shrink(f) + bias + part).astype(BF)

    locals_["dg"].wait()
    locals_["ds"].wait()

    def target(group, f):
        return dg[group, t * H + f]

    def rank(group, f):
        return sum((jnp.int32(target(group, e) == target(group, f)) for e in range(f)), jnp.int32(0))

    for j in range(n_clips - 1):
        group = lax.rem(g + 1 + j, n_clips)
        for slot in range(2):
            frame = jnp.int32(0)
            for f in range(H):
                mine = jnp.logical_and(target(g, f) == group, rank(g, f) == slot)
                frame = jnp.where(mine, f, frame)
            sel[j, slot] = red[frame]
    for j in (1, 0, 2):
        send(("x", j), sel.at[j], got.at[pl.ds(2 * j, 2)], others[j])
    for f in range(H):
        got[6 + f] = red[f]

    place = [jnp.int32(-1)] * H
    for j in range(n_clips):
        group = g if j == n_clips - 1 else lax.rem(g + n_clips - 1 - j, n_clips)
        for f in range(H):
            slot = jnp.int32(f) if j == n_clips - 1 else rank(group, f)
            here = target(group, f) == g
            position = ds[group, t * H + f]
            for p in range(H):
                place[p] = jnp.where(jnp.logical_and(here, position == p), 2 * j + slot, place[p])
    locals_["p"].wait()
    for j in range(n_clips - 1):
        arrived(("x", j))
    for p in range(H):
        x = got[jnp.maximum(place[p], 0)]
        y = dot(pw[...], x) + jnp.concatenate([pcol[...], pcol[...]], axis=1)
        y = jnp.where(place[p] >= 0, y, 0.0)
        out[p] = y.reshape(C2, 2, HALF).astype(BF)
    for copy in copies.values():
        copy.wait_send()


N_COPIES, N_FETCHES = 28, 16


def local(
    video, norm1_gain, conv1_weight, conv1_bias, norm2_gain, conv2_weight, conv2_bias,
    down_weight, down_bias, proj_weight, proj_bias, dest_group, dest_slot, sizes,
):
    vm = pl.BlockSpec(memory_space=pltpu.VMEM)
    hbm = pl.BlockSpec(memory_space=pltpu.HBM)
    row = lambda v: v.reshape(1, C)
    taps = 9 * C
    packed = pl.pallas_call(
        functools.partial(kernel, sizes),
        out_shape=jax.ShapeDtypeStruct((H, C2, 2, HALF), BF),
        in_specs=[hbm] * 13,
        out_specs=vm,
        scratch_shapes=[
            pltpu.VMEM((H, C, H, W), BF),
            pltpu.VMEM((C, H, W), BF),
            pltpu.VMEM((H, C, W), BF),
            pltpu.VMEM((H, H, C, W), BF),
            pltpu.VMEM((H, C, W), BF),
            pltpu.VMEM((H + 1, H + 2, C, W), BF),
            pltpu.VMEM((H, H + 3, C, W), BF),
            pltpu.VMEM((H, C, W), BF),
            pltpu.VMEM((H, C, W), BF),
            pltpu.VMEM((H, H + 1, 3, C, HALF), BF),
            pltpu.VMEM((H, C, W), BF),
            pltpu.VMEM((2, C, W), BF),
            pltpu.VMEM((2, C, W), BF),
            pltpu.VMEM((3, 2, C, W), BF),
            pltpu.VMEM((10, C, W), BF),
            pltpu.VMEM((9, 3 * C, C), BF),
            pltpu.VMEM((9, 3 * C, C), BF),
            pltpu.VMEM((9, C, C), BF),
            pltpu.VMEM((C2, C), BF),
            pltpu.VMEM((3 * C, taps), BF),
            pltpu.VMEM((3 * C, 6 * C), BF),
            pltpu.VMEM((3 * C, 3 * C), BF),
            pltpu.VMEM((3 * C, taps), BF),
            pltpu.VMEM((3 * C, 6 * C), BF),
            pltpu.VMEM((3 * C, 3 * C), BF),
            pltpu.VMEM((3 * C, 3 * C), BF),
            pltpu.VMEM((3 * C, 6 * C), BF),
            pltpu.VMEM((C, taps), BF),
            pltpu.VMEM((W, W), BF),
            pltpu.VMEM((5, 1, C), F32),
            pltpu.VMEM((1, C2), F32),
            pltpu.VMEM((5, C, HALF), F32),
            pltpu.VMEM((C2, HALF), F32),
            pltpu.SMEM((4, 32), jnp.int32),
            pltpu.SMEM((4, 32), jnp.int32),
            pltpu.SemaphoreType.DMA((N_FETCHES,)),
            pltpu.SemaphoreType.DMA((N_COPIES,)),
            pltpu.SemaphoreType.DMA((N_COPIES,)),
        ],
        compiler_params=pltpu.CompilerParams(
            collective_id=0, has_side_effects=True, vmem_limit_bytes=63 << 20
        ),
        cost_estimate=pl.CostEstimate(flops=5 * 10**9, bytes_accessed=3 << 20, transcendentals=1 << 20),
        name="encode",
    )(
        dest_group, dest_slot, video[0], row(norm1_gain), row(conv1_bias), row(norm2_gain),
        row(conv2_bias), row(down_bias), proj_bias.reshape(1, C2),
        conv1_weight.reshape(9, 3 * C, C), conv2_weight.reshape(9, 3 * C, C),
        down_weight.reshape(9, C, C), proj_weight,
    )
    return packed[None, None]


def solution(mesh):
    sizes = (mesh.shape["clips"], mesh.shape["tm"], mesh.shape["tile"])
    return jax.shard_map(
        functools.partial(local, sizes=sizes),
        mesh=mesh,
        in_specs=(P("clips", "tm", None, "tile", None),) + (P(),) * 12,
        out_specs=P("clips", "tm", None, None, "tile", None),
        check_vma=False,
    )
```

profile of v0, /device:TPU:1, one launch (start us, length us, event | category | flops | bytes accessed | tf_op | source)
XLA Modules:
  0.0 45.6 jit_solution(4184674555308659547)
XLA Ops:
  0.0 43.5 %encode.1 = bf16[4,192,2,128]{3,2,1,0:T(2,128)(2,1)} custom-call(s32[4,32]{1,0:T(4,128)} %dgh.1, s32[4,32]{1,0:T(4,128)} %dsh.1, bf16[4,96,4,256]{3,2,1,0:T(4,128)(2,1)} %bitcast.12, f32[1,96]{1,0:T(1,128)} %bitcast.17, f32[1,96]{1,0:T(1,128)} %bitcast.18, f32[1,96]{1,0:T(1,128)} %bitcast.19, f32[1,96]{1,0:T(1,128)} %bitcast.20, f32[1,96]{1,0:T(1,128)} %bitcast.21, ...), custom_call_target="tpu_custom_call" | custom-call | flops 5000000000 | bytes 3145728 | tf_op jit(solution)/shard_map/encode/pallas_call | solution.py:323
  43.5 2.0 %copy.15 = bf16[1,1,4,192,2,128]{5,4,3,2,1,0:T(2,128)(2,1)} copy(bf16[1,1,4,192,2,128]{5,4,3,2,1,0:T(2,128)(2,1)} %bitcast.11) | data formatting | bytes 786432
where the time goes:
time: 45.7 us; the launch traced here: 45.6 us
  Pallas kernels  43.5 us (95%)
  local copies, waits for them, and re-layouts  2.01 us (4%)
    pallas_call x1, Pallas kernels, local(): pl.pallas_call(functools.partial(kernel, sizes), out_shape=jax.ShapeDtype...  43.5 us
    unnamed x1, local copies, waits for them, and re-layouts  2.01 us

commit v1 on v0

v1 whole, which is shorter than its diff:
```python
import functools

import jax
import jax.numpy as jnp
from jax import lax
from jax.experimental import pallas as pl
from jax.experimental.pallas import tpu as pltpu
from jax.sharding import PartitionSpec as P

MESH = pl.DeviceIdType.MESH
EPS = 1e-06
C, C2, H, W, HALF = 96, 192, 4, 256, 128
BF, F32 = jnp.bfloat16, jnp.float32


def dot(a, b):
    return jnp.dot(a, b, preferred_element_type=F32)


def kernel(
    sizes,
    dgh, dsh, video, g1h, b1h, g2h, b2h, bdh, bph, w1h, w2h, dh, ph,
    out,
    vraw, vh, vht, vt, vn, a1, a2, s_out, s_in, bl, red, p_out, p_in, sel, got,
    w1raw, w2raw, draw, pw, w1f, w1m, w1e, w2f, w2m, w2l, w2e, w2p, dw,
    perm, rows, prow, cols, pcol, dg, ds, lsem, ssem, rsem,
):
    n_clips, n_tm, n_tile = sizes
    g = lax.axis_index("clips")
    t = lax.axis_index("tm")
    k = lax.axis_index("tile")
    top, bottom = k == 0, k == n_tile - 1
    first, last = t == 0, t == n_tm - 1
    up = ("tile", jnp.maximum(k - 1, 0), k > 0, k < n_tile - 1)
    down = ("tile", jnp.minimum(k + 1, n_tile - 1), k < n_tile - 1, k > 0)
    later = ("tm", jnp.minimum(t + 1, n_tm - 1), t < n_tm - 1, t > 0)
    before = ("tm", jnp.maximum(t - 1, 0), t > 0, t < n_tm - 1)
    others = [("clips", lax.rem(g + 1 + j, n_clips), None, None) for j in range(n_clips - 1)]

    def under(condition, act):
        if condition is None:
            act()
        else:
            pl.when(condition)(act)

    copies = {}

    def send(name, src, dst, way):
        axis, coordinate, sends, receives = way
        i = len(copies)
        copy = pltpu.make_async_remote_copy(
            src_ref=src, dst_ref=dst, send_sem=ssem.at[i], recv_sem=rsem.at[i],
            device_id={axis: coordinate}, device_id_type=MESH,
        )
        under(sends, copy.start)
        copies[name] = (copy, sends, receives)

    def arrived(name):
        copy, _, receives = copies[name]
        under(receives, copy.wait_recv)

    fetches = {}

    def fetch(name, src, dst):
        copy = pltpu.make_async_copy(src, dst, lsem.at[len(fetches)])
        copy.start()
        fetches[name] = copy

    barrier = pltpu.get_barrier_semaphore()
    for axis, coordinate, sends, _ in [up, down, later, before] + others:
        under(sends, functools.partial(
            pl.semaphore_signal, barrier, inc=1, device_id={axis: coordinate}, device_id_type=MESH
        ))
    for f in (2, 3, 1, 0):
        fetch(("v", f), video.at[f], vraw.at[f])
    for i, vector in enumerate((g1h, b1h, g2h, b2h, bdh)):
        fetch(("row", i), vector, rows.at[i])
    fetch("prow", bph, prow)
    fetch("w1", w1h, w1raw)
    fetch("w2", w2h, w2raw)
    fetch("d", dh, draw)
    fetch("p", ph, pw)
    fetch("dg", dgh, dg)
    fetch("ds", dsh, ds)

    @pl.when(top)
    def _():
        for f in range(H + 1):
            a1[f, 0] = jnp.zeros((C, W), BF)
        for f in range(H):
            a2[f, 0] = jnp.zeros((C, W), BF)

    @pl.when(bottom)
    def _():
        for f in range(H + 1):
            a1[f, 5] = jnp.zeros((C, W), BF)
        for f in range(H):
            a2[f, pl.ds(5, 2)] = jnp.zeros((2, C, W), BF)
            vn[f] = jnp.zeros((C, W), BF)

    @pl.when(first)
    def _():
        vh[...] = jnp.zeros(vh.shape, BF)
        s_in[...] = jnp.zeros(s_in.shape, BF)
        p_in[...] = jnp.zeros(p_in.shape, BF)

    src_col = lax.broadcasted_iota(jnp.int32, (W, W), 0)
    dst_col = lax.broadcasted_iota(jnp.int32, (W, W), 1)
    want = jnp.where(dst_col < HALF, 2 * dst_col, 2 * dst_col - (W - 1))
    perm[...] = (src_col == want).astype(F32).astype(BF)

    pl.semaphore_wait(
        barrier,
        len(others) + jnp.int32(k > 0) + jnp.int32(k < n_tile - 1) + jnp.int32(t > 0) + jnp.int32(t < n_tm - 1),
    )
    send("v", video.at[3], vh, later)

    def column(row):
        n = row.shape[1]
        eye = lax.broadcasted_iota(jnp.int32, (n, n), 0) == lax.broadcasted_iota(jnp.int32, (n, n), 1)
        col = jnp.sum(jnp.where(eye, row, 0.0), axis=1, keepdims=True)
        return jnp.broadcast_to(col, (n, HALF))

    for i in range(5):
        fetches[("row", i)].wait()
    for i in range(5):
        cols[i] = column(rows[i])

    lane = lax.broadcasted_iota(jnp.int32, (C, HALF), 1)

    def halves(x):
        return x[:, :HALF], x[:, HALF:]

    def norm_silu(x, gain):
        ms = jnp.sum(x * x, axis=0, keepdims=True) * (1.0 / C)
        n = x * (lax.rsqrt(ms + EPS) * 0.5) * gain
        return n + n * jnp.tanh(n)

    def conv_row(a, frames, w, r):
        x = jnp.concatenate([a[f, pl.ds(r, 3)].reshape(3 * C, W) for f in frames], axis=0)
        y = dot(w[...], x)
        y0e, y0o = halves(y[:C])
        y1e, y1o = halves(y[C : 2 * C])
        y2e, y2o = halves(y[2 * C :])
        even = y1e + y2o + jnp.where(lane == 0, 0.0, pltpu.roll(y0o, 1, 1))
        odd = y1o + y0e + jnp.where(lane == HALF - 1, 0.0, pltpu.roll(y2e, HALF - 1, 1))
        return even, odd

    def turn(raw, dst):
        v = jnp.swapaxes(raw, 0, 1).reshape(H * C, W)
        dst[...] = dot(v, perm[...]).astype(BF).reshape(H, C, W)

    def first_act(src, index):
        for r in range(H):
            for side in range(2):
                s = pl.ds(HALF * side, HALF)
                a1[index, r + 1, :, s] = norm_silu(src[r, :, s].astype(F32), cols[0]).astype(BF)

    def send_a1(i):
        send(("a1up", i), a1.at[i, 1], a1.at[i, 5], up)
        send(("a1down", i), a1.at[i, 4], a1.at[i, 0], down)

    def take_a1(i):
        arrived(("a1up", i))
        arrived(("a1down", i))

    def send_a2(f):
        send(("a2up", f), a2.at[f, pl.ds(1, 2)], a2.at[f, pl.ds(5, 2)], up)
        send(("a2down", f), a2.at[f, 4], a2.at[f, 0], down)

    def second_act(f, r, even, odd):
        for side, x in enumerate((even, odd)):
            x = (x + cols[1]).astype(BF).astype(F32)
            a2[f, r + 1, :, pl.ds(HALF * side, HALF)] = norm_silu(x, cols[2]).astype(BF)

    for f in (2, 3, 1, 0):
        fetches[("v", f)].wait()
        turn(vraw[f], vt.at[f])
        first_act(vt.at[f], f + 1)
        send_a1(f + 1)
        send(("vt", f), vt.at[f, 0], vn.at[f], up)

    def gather_taps(raw, taps):
        return jnp.concatenate([raw[3 * i + j] for i in taps for j in range(3)], axis=1)

    fetches["w1"].wait()
    w1e[...] = gather_taps(w1raw, (0,))
    w1f[...] = gather_taps(w1raw, (0, 1, 2))
    w1m[...] = gather_taps(w1raw, (1, 2))

    take_a1(3)
    for r in range(H):
        even, odd = conv_row(a1, (3,), w1e, r)
        s_out[r, :, pl.ds(0, HALF)] = even.astype(BF)
        s_out[r, :, pl.ds(HALF, HALF)] = odd.astype(BF)
    send("s", s_out, s_in, later)

    take_a1(4)
    take_a1(2)
    for r in (0, 1, 3):
        second_act(3, r, *conv_row(a1, (2, 3, 4), w1f, r))
    send_a2(3)
    second_act(3, 2, *conv_row(a1, (2, 3, 4), w1f, 2))
    take_a1(1)
    for r in (0, 1, 3):
        second_act(2, r, *conv_row(a1, (1, 2, 3), w1f, r))
    send_a2(2)
    second_act(2, 2, *conv_row(a1, (1, 2, 3), w1f, 2))

    arrived("v")
    turn(vh[...], vht)
    first_act(vht, 0)
    send_a1(0)

    fetches["w2"].wait()
    w2f[...] = gather_taps(w2raw, (0, 1, 2))
    w2p[...] = gather_taps(w2raw, (0, 1))
    w2m[...] = gather_taps(w2raw, (1, 2))
    w2e[...] = gather_taps(w2raw, (0,))
    w2l[...] = gather_taps(w2raw, (2,))
    fetches["d"].wait()
    dw[...] = jnp.concatenate([draw[i] for i in range(9)], axis=1)
    for r in (1, 2):
        second_act(1, r, *conv_row(a1, (0, 1, 2), w1f, r))

    def block_row(slot, r, even, odd):
        if r == H:
            even = jnp.where(bottom, 0.0, even)
            odd = jnp.where(bottom, 0.0, odd)
        even = even.astype(BF).astype(F32)
        bl[slot, r, 0] = even.astype(BF)
        bl[slot, r, 1] = odd.astype(BF)
        bl[slot, r, 2] = jnp.where(lane == HALF - 1, 0.0, pltpu.roll(even, HALF - 1, 1)).astype(BF)

    def shrink(slots, q):
        x = jnp.concatenate([bl[i, pl.ds(2 * q, 3)].reshape(9 * C, HALF) for i in slots], axis=1)
        return halves(dot(dw[...], x))

    for f in (3, 2):
        arrived(("a2up", f))
        arrived(("a2down", f))
    for r in range(H + 1):
        block_row(4, r, *conv_row(a2, (2, 3), w2p, r))
        block_row(5, r, *conv_row(a2, (3,), w2e, r))
    for q in range(2):
        for i, part in enumerate(shrink((4, 5), q)):
            p_out[q, i] = part.astype(BF)
    send("p", p_out, p_in, later)

    take_a1(0)
    for r in (0, 3):
        second_act(1, r, *conv_row(a1, (0, 1, 2), w1f, r))
    send_a2(1)

    def first_frame(r):
        even, odd = conv_row(a1, (0, 1), w1m, r)
        se, so = halves(s_in[r].astype(F32))
        second_act(0, r, even + se, odd + so)

    arrived("s")
    for r in (0, 1, 3):
        first_frame(r)
    send_a2(0)
    first_frame(2)

    fetches["dg"].wait()
    fetches["ds"].wait()

    def target(group, f):
        return dg[group, t * H + f]

    def rank(group, f):
        return sum((jnp.int32(target(group, e) == target(group, f)) for e in range(f)), jnp.int32(0))

    picks = []
    own = [(target(g, f), rank(g, f)) for f in range(H)]
    for j in range(n_clips - 1):
        group = lax.rem(g + 1 + j, n_clips)
        for slot in range(2):
            frame = jnp.int32(0)
            for f, (to, order) in enumerate(own):
                frame = jnp.where(jnp.logical_and(to == group, order == slot), f, frame)
            picks.append(frame)
    place = [jnp.int32(-1)] * H
    for j in range(n_clips):
        mine = j == n_clips - 1
        group = g if mine else lax.rem(g + n_clips - 1 - j, n_clips)
        for f in range(H):
            slot = jnp.int32(f) if mine else rank(group, f)
            here = target(group, f) == g
            position = ds[group, t * H + f]
            for p in range(H):
                place[p] = jnp.where(jnp.logical_and(here, position == p), 2 * j + slot, place[p])

    for f in range(H):
        arrived(("vt", f))

    def block(f, r):
        frames, w = {3: ((1, 2, 3), w2f), 2: ((0, 1, 2), w2f), 1: ((0, 1), w2m), 0: ((0,), w2l)}[f]
        even, odd = conv_row(a2, frames, w, r)
        ve, vo = halves((vt[f, r] if r < H else vn[f]).astype(F32))
        block_row(f, r, even + cols[3] + ve, odd + cols[3] + vo)

    def ship(q):
        for pair in ((3, 2), (1, 0)):
            for f, part in zip(pair, shrink(pair, q)):
                if f < 2:
                    part = part + p_in[q, f].astype(F32)
                part = (part + cols[4]).astype(BF)
                red[q, f] = part
                got[q, 6 + f] = part
        for j in range(n_clips - 1):
            for slot in range(2):
                sel[q, j, slot] = red[q, picks[2 * j + slot]]
        for j in (1, 0, 2):
            send(("x", q, j), sel.at[q, j], got.at[q, pl.ds(2 * j, 2)], others[j])

    for r in (1, 2):
        for f in (3, 2, 1, 0):
            block(f, r)
    arrived(("a2down", 1))
    arrived(("a2down", 0))
    for f in (3, 2, 1, 0):
        block(f, 0)
    arrived("p")
    ship(0)
    arrived(("a2up", 1))
    arrived(("a2up", 0))
    for r in (3, 4):
        for f in (3, 2, 1, 0):
            block(f, r)
    ship(1)

    fetches["prow"].wait()
    pcol[...] = column(prow[...])
    fetches["p"].wait()
    for q in range(2):
        for j in range(n_clips - 1):
            arrived(("x", q, j))
    bias = jnp.concatenate([pcol[...], pcol[...]], axis=1)
    for p in range(H):
        i = jnp.maximum(place[p], 0)
        y = dot(pw[...], jnp.concatenate([got[0, i], got[1, i]], axis=1)) + bias
        y = jnp.where(place[p] >= 0, y, 0.0)
        out[p] = y.reshape(C2, 2, HALF).astype(BF)
    for copy, sends, _ in copies.values():
        under(sends, copy.wait_send)


N_COPIES, N_FETCHES = 31, 16


def local(
    video, norm1_gain, conv1_weight, conv1_bias, norm2_gain, conv2_weight, conv2_bias,
    down_weight, down_bias, proj_weight, proj_bias, dest_group, dest_slot, sizes,
):
    vm = pl.BlockSpec(memory_space=pltpu.VMEM)
    hbm = pl.BlockSpec(memory_space=pltpu.HBM)
    row = lambda v: v.reshape(1, C)
    taps = 9 * C
    packed = pl.pallas_call(
        functools.partial(kernel, sizes),
        out_shape=jax.ShapeDtypeStruct((H, C2, 2, HALF), BF),
        in_specs=[hbm] * 13,
        out_specs=vm,
        scratch_shapes=[
            pltpu.VMEM((H, C, H, W), BF),
            pltpu.VMEM((C, H, W), BF),
            pltpu.VMEM((H, C, W), BF),
            pltpu.VMEM((H, H, C, W), BF),
            pltpu.VMEM((H, C, W), BF),
            pltpu.VMEM((H + 1, H + 2, C, W), BF),
            pltpu.VMEM((H, H + 3, C, W), BF),
            pltpu.VMEM((H, C, W), BF),
            pltpu.VMEM((H, C, W), BF),
            pltpu.VMEM((H + 2, H + 1, 3, C, HALF), BF),
            pltpu.VMEM((2, H, C, HALF), BF),
            pltpu.VMEM((2, 2, C, HALF), BF),
            pltpu.VMEM((2, 2, C, HALF), BF),
            pltpu.VMEM((2, 3, 2, C, HALF), BF),
            pltpu.VMEM((2, 10, C, HALF), BF),
            pltpu.VMEM((9, 3 * C, C), BF),
            pltpu.VMEM((9, 3 * C, C), BF),
            pltpu.VMEM((9, C, C), BF),
            pltpu.VMEM((C2, C), BF),
            pltpu.VMEM((3 * C, taps), BF),
            pltpu.VMEM((3 * C, 6 * C), BF),
            pltpu.VMEM((3 * C, 3 * C), BF),
            pltpu.VMEM((3 * C, taps), BF),
            pltpu.VMEM((3 * C, 6 * C), BF),
            pltpu.VMEM((3 * C, 3 * C), BF),
            pltpu.VMEM((3 * C, 3 * C), BF),
            pltpu.VMEM((3 * C, 6 * C), BF),
            pltpu.VMEM((C, taps), BF),
            pltpu.VMEM((W, W), BF),
            pltpu.VMEM((5, 1, C), F32),
            pltpu.VMEM((1, C2), F32),
            pltpu.VMEM((5, C, HALF), F32),
            pltpu.VMEM((C2, HALF), F32),
            pltpu.SMEM((4, 32), jnp.int32),
            pltpu.SMEM((4, 32), jnp.int32),
            pltpu.SemaphoreType.DMA((N_FETCHES,)),
            pltpu.SemaphoreType.DMA((N_COPIES,)),
            pltpu.SemaphoreType.DMA((N_COPIES,)),
        ],
        compiler_params=pltpu.CompilerParams(
            collective_id=0, has_side_effects=True, vmem_limit_bytes=63 << 20
        ),
        cost_estimate=pl.CostEstimate(flops=5 * 10**9, bytes_accessed=3 << 20, transcendentals=1 << 20),
        name="encode",
    )(
        dest_group, dest_slot, video[0], row(norm1_gain), row(conv1_bias), row(norm2_gain),
        row(conv2_bias), row(down_bias), proj_bias.reshape(1, C2),
        conv1_weight.reshape(9, 3 * C, C), conv2_weight.reshape(9, 3 * C, C),
        down_weight.reshape(9, C, C), proj_weight,
    )
    return packed[None, None]


def solution(mesh):
    sizes = (mesh.shape["clips"], mesh.shape["tm"], mesh.shape["tile"])
    return jax.shard_map(
        functools.partial(local, sizes=sizes),
        mesh=mesh,
        in_specs=(P("clips", "tm", None, "tile", None),) + (P(),) * 12,
        out_specs=P("clips", "tm", None, None, "tile", None),
        check_vma=False,
    )
```

time: 45.7 us -> 34.5 us (0.75)
  the two profiles are of different devices: /device:TPU:1 before, /device:TPU:217 now
where the time goes in v1:
time: 34.5 us; the launch traced here: 34.3 us
  Pallas kernels  32.3 us (94%)
  local copies, waits for them, and re-layouts  2.01 us (6%)
    pallas_call x1, Pallas kernels, local(): pl.pallas_call(functools.partial(kernel, sizes), out_shape=jax.ShapeDtype...  32.3 us
    unnamed x1, local copies, waits for them, and re-layouts  2.01 us

profile of v1, /device:TPU:217, one launch (start us, length us, event | category | flops | bytes accessed | tf_op | source)
XLA Modules:
  0.0 34.3 jit_solution(3142789811740844849)
XLA Ops:
  0.0 32.3 %encode.1 = bf16[4,192,2,128]{3,2,1,0:T(2,128)(2,1)} custom-call(s32[4,32]{1,0:T(4,128)} %dgh.1, s32[4,32]{1,0:T(4,128)} %dsh.1, bf16[4,96,4,256]{3,2,1,0:T(4,128)(2,1)} %bitcast.12, f32[1,96]{1,0:T(1,128)} %bitcast.17, f32[1,96]{1,0:T(1,128)} %bitcast.18, f32[1,96]{1,0:T(1,128)} %bitcast.19, f32[1,96]{1,0:T(1,128)} %bitcast.20, f32[1,96]{1,0:T(1,128)} %bitcast.21, ...), custom_call_target="tpu_custom_call" | custom-call | flops 5000000000 | bytes 3145728 | tf_op jit(solution)/shard_map/encode/pallas_call | solution.py:361
  32.3 2.0 %copy.15 = bf16[1,1,4,192,2,128]{5,4,3,2,1,0:T(2,128)(2,1)} copy(bf16[1,1,4,192,2,128]{5,4,3,2,1,0:T(2,128)(2,1)} %bitcast.11) | data formatting | bytes 786432

commit v2 on v1

--- a/solution.py
+++ b/solution.py
@@ -17,13 +17,20 @@
     return jnp.dot(a, b, preferred_element_type=F32)
 
 
+def column(row):
+    n = row.shape[1]
+    eye = lax.broadcasted_iota(jnp.int32, (n, n), 0) == lax.broadcasted_iota(jnp.int32, (n, n), 1)
+    col = jnp.sum(jnp.where(eye, row, 0.0), axis=1, keepdims=True)
+    return jnp.broadcast_to(col, (n, HALF))
+
+
 def kernel(
     sizes,
-    dgh, dsh, video, g1h, b1h, g2h, b2h, bdh, bph, w1h, w2h, dh, ph,
+    dgh, dsh, video, g1h, b1h, g2h, b2h, bdh, w1h, w2h, dh,
     out,
-    vraw, vh, vht, vt, vn, a1, a2, s_out, s_in, bl, red, p_out, p_in, sel, got,
-    w1raw, w2raw, draw, pw, w1f, w1m, w1e, w2f, w2m, w2l, w2e, w2p, dw,
-    perm, rows, prow, cols, pcol, dg, ds, lsem, ssem, rsem,
+    vraw, vh, vht, vt, vn, a1, a2, s_out, s_in, part, bl, red, p_out, p_in, sel, got,
+    w1raw, w2raw, draw, w1f, w1m, w1e, w2f, w2m, w2l, w2e, w2p, dw,
+    perm, rows, cols, dg, ds, lsem, ssem, rsem,
 ):
     n_clips, n_tm, n_tile = sizes
     g = lax.axis_index("clips")
@@ -31,11 +38,14 @@
     k = lax.axis_index("tile")
     top, bottom = k == 0, k == n_tile - 1
     first, last = t == 0, t == n_tm - 1
-    up = ("tile", jnp.maximum(k - 1, 0), k > 0, k < n_tile - 1)
-    down = ("tile", jnp.minimum(k + 1, n_tile - 1), k < n_tile - 1, k > 0)
-    later = ("tm", jnp.minimum(t + 1, n_tm - 1), t < n_tm - 1, t > 0)
-    before = ("tm", jnp.maximum(t - 1, 0), t > 0, t < n_tm - 1)
-    others = [("clips", lax.rem(g + 1 + j, n_clips), None, None) for j in range(n_clips - 1)]
+    ways = {
+        "up": ("tile", jnp.maximum(k - 1, 0), k > 0, k < n_tile - 1),
+        "down": ("tile", jnp.minimum(k + 1, n_tile - 1), k < n_tile - 1, k > 0),
+        "later": ("tm", jnp.minimum(t + 1, n_tm - 1), t < n_tm - 1, t > 0),
+        "before": ("tm", jnp.maximum(t - 1, 0), t > 0, t < n_tm - 1),
+    }
+    for j in range(n_clips - 1):
+        ways[j] = ("clips", lax.rem(g + 1 + j, n_clips), None, None)
 
     def under(condition, act):
         if condition is None:
@@ -45,19 +55,37 @@
 
     copies = {}
 
-    def send(name, src, dst, way):
-        axis, coordinate, sends, receives = way
-        i = len(copies)
-        copy = pltpu.make_async_remote_copy(
-            src_ref=src, dst_ref=dst, send_sem=ssem.at[i], recv_sem=rsem.at[i],
-            device_id={axis: coordinate}, device_id_type=MESH,
-        )
-        under(sends, copy.start)
-        copies[name] = (copy, sends, receives)
-
-    def arrived(name):
-        copy, _, receives = copies[name]
-        under(receives, copy.wait_recv)
+    def send(way, **parts):
+        axis, coordinate, sends, _ = ways[way]
+        group = []
+        for name, (src, dst) in parts.items():
+            i = len(copies)
+            copy = pltpu.make_async_remote_copy(
+                src_ref=src, dst_ref=dst, send_sem=ssem.at[i], recv_sem=rsem.at[i],
+                device_id={axis: coordinate}, device_id_type=MESH,
+            )
+            copies[name] = (copy, way)
+            group.append(copy)
+
+        def start():
+            for copy in group:
+                copy.start()
+
+        under(sends, start)
+
+    def each_way(names, side, act):
+        for way in ways:
+            group = [copies[name][0] for name in names if copies[name][1] == way]
+
+            def run(group=group):
+                for copy in group:
+                    act(copy)
+
+            if group:
+                under(ways[way][side], run)
+
+    def arrived(*names):
+        each_way(names, 3, lambda copy: copy.wait_recv())
 
     fetches = {}
 
@@ -67,7 +95,7 @@
         fetches[name] = copy
 
     barrier = pltpu.get_barrier_semaphore()
-    for axis, coordinate, sends, _ in [up, down, later, before] + others:
+    for axis, coordinate, sends, _ in ways.values():
         under(sends, functools.partial(
             pl.semaphore_signal, barrier, inc=1, device_id={axis: coordinate}, device_id_type=MESH
         ))
@@ -75,11 +103,9 @@
         fetch(("v", f), video.at[f], vraw.at[f])
     for i, vector in enumerate((g1h, b1h, g2h, b2h, bdh)):
         fetch(("row", i), vector, rows.at[i])
-    fetch("prow", bph, prow)
     fetch("w1", w1h, w1raw)
     fetch("w2", w2h, w2raw)
     fetch("d", dh, draw)
-    fetch("p", ph, pw)
     fetch("dg", dgh, dg)
     fetch("ds", dsh, ds)
 
@@ -111,15 +137,9 @@
 
     pl.semaphore_wait(
         barrier,
-        len(others) + jnp.int32(k > 0) + jnp.int32(k < n_tile - 1) + jnp.int32(t > 0) + jnp.int32(t < n_tm - 1),
+        n_clips - 1 + jnp.int32(k > 0) + jnp.int32(k < n_tile - 1) + jnp.int32(t > 0) + jnp.int32(t < n_tm - 1),
     )
-    send("v", video.at[3], vh, later)
-
-    def column(row):
-        n = row.shape[1]
-        eye = lax.broadcasted_iota(jnp.int32, (n, n), 0) == lax.broadcasted_iota(jnp.int32, (n, n), 1)
-        col = jnp.sum(jnp.where(eye, row, 0.0), axis=1, keepdims=True)
-        return jnp.broadcast_to(col, (n, HALF))
+    send("later", v=(video.at[3], vh))
 
     for i in range(5):
         fetches[("row", i)].wait()
@@ -156,29 +176,29 @@
                 s = pl.ds(HALF * side, HALF)
                 a1[index, r + 1, :, s] = norm_silu(src[r, :, s].astype(F32), cols[0]).astype(BF)
 
-    def send_a1(i):
-        send(("a1up", i), a1.at[i, 1], a1.at[i, 5], up)
-        send(("a1down", i), a1.at[i, 4], a1.at[i, 0], down)
-
-    def take_a1(i):
-        arrived(("a1up", i))
-        arrived(("a1down", i))
-
-    def send_a2(f):
-        send(("a2up", f), a2.at[f, pl.ds(1, 2)], a2.at[f, pl.ds(5, 2)], up)
-        send(("a2down", f), a2.at[f, 4], a2.at[f, 0], down)
+    def send_a1(first, count):
+        i = pl.ds(first, count)
+        send("down", **{f"a1down{first}": (a1.at[i, 4], a1.at[i, 0])})
+        send("up", **{f"a1up{first}": (a1.at[i, 1], a1.at[i, 5])})
+
+    def send_a2(first, count):
+        f = pl.ds(first, count)
+        send("down", **{f"a2down{first}": (a2.at[f, 4], a2.at[f, 0])})
+        send("up", **{f"a2up{first}": (a2.at[f, pl.ds(1, 2)], a2.at[f, pl.ds(5, 2)])})
 
     def second_act(f, r, even, odd):
         for side, x in enumerate((even, odd)):
             x = (x + cols[1]).astype(BF).astype(F32)
             a2[f, r + 1, :, pl.ds(HALF * side, HALF)] = norm_silu(x, cols[2]).astype(BF)
 
-    for f in (2, 3, 1, 0):
-        fetches[("v", f)].wait()
-        turn(vraw[f], vt.at[f])
-        first_act(vt.at[f], f + 1)
-        send_a1(f + 1)
-        send(("vt", f), vt.at[f, 0], vn.at[f], up)
+    for pair in ((2, 3), (0, 1)):
+        for f in pair:
+            fetches[("v", f)].wait()
+        for f in pair:
+            turn(vraw[f], vt.at[f])
+            first_act(vt.at[f], f + 1)
+        send_a1(pair[0] + 1, 2)
+    send("up", vt=(vt.at[:, 0], vn))
 
     def gather_taps(raw, taps):
         return jnp.concatenate([raw[3 * i + j] for i in taps for j in range(3)], axis=1)
@@ -188,40 +208,44 @@
     w1f[...] = gather_taps(w1raw, (0, 1, 2))
     w1m[...] = gather_taps(w1raw, (1, 2))
 
-    take_a1(3)
-    for r in range(H):
+    def early_tap(r):
         even, odd = conv_row(a1, (3,), w1e, r)
-        s_out[r, :, pl.ds(0, HALF)] = even.astype(BF)
-        s_out[r, :, pl.ds(HALF, HALF)] = odd.astype(BF)
-    send("s", s_out, s_in, later)
-
-    take_a1(4)
-    take_a1(2)
-    for r in (0, 1, 3):
+        i = (2, 0, 1, 3)[r]
+        s_out[i, :, pl.ds(0, HALF)] = even.astype(BF)
+        s_out[i, :, pl.ds(HALF, HALF)] = odd.astype(BF)
+
+    for r in (1, 2):
+        early_tap(r)
+    for r in (1, 2):
         second_act(3, r, *conv_row(a1, (2, 3, 4), w1f, r))
-    send_a2(3)
-    second_act(3, 2, *conv_row(a1, (2, 3, 4), w1f, 2))
-    take_a1(1)
-    for r in (0, 1, 3):
         second_act(2, r, *conv_row(a1, (1, 2, 3), w1f, r))
-    send_a2(2)
-    second_act(2, 2, *conv_row(a1, (1, 2, 3), w1f, 2))
-
-    arrived("v")
-    turn(vh[...], vht)
-    first_act(vht, 0)
-    send_a1(0)
-
+    send("later", s0=(s_out.at[pl.ds(0, 2)], s_in.at[pl.ds(0, 2)]))
     fetches["w2"].wait()
+    fetches["d"].wait()
     w2f[...] = gather_taps(w2raw, (0, 1, 2))
     w2p[...] = gather_taps(w2raw, (0, 1))
     w2m[...] = gather_taps(w2raw, (1, 2))
     w2e[...] = gather_taps(w2raw, (0,))
     w2l[...] = gather_taps(w2raw, (2,))
-    fetches["d"].wait()
     dw[...] = jnp.concatenate([draw[i] for i in range(9)], axis=1)
+
+    arrived("a1down3", "a1up3", "a1down1", "a1up1")
+    for r in (0, 3):
+        early_tap(r)
+    for r in (0, 3):
+        second_act(3, r, *conv_row(a1, (2, 3, 4), w1f, r))
+        second_act(2, r, *conv_row(a1, (1, 2, 3), w1f, r))
+    send("later", s1=(s_out.at[pl.ds(2, 2)], s_in.at[pl.ds(2, 2)]))
+    send_a2(2, 2)
+
+    arrived("v")
+    turn(vh[...], vht)
+    first_act(vht, 0)
+    send_a1(0, 1)
+
     for r in (1, 2):
         second_act(1, r, *conv_row(a1, (0, 1, 2), w1f, r))
+        part[r - 1, 0], part[r - 1, 1] = conv_row(a1, (0, 1), w1m, r)
 
     def block_row(slot, r, even, odd):
         if r == H:
@@ -236,32 +260,34 @@
         x = jnp.concatenate([bl[i, pl.ds(2 * q, 3)].reshape(9 * C, HALF) for i in slots], axis=1)
         return halves(dot(dw[...], x))
 
-    for f in (3, 2):
-        arrived(("a2up", f))
-        arrived(("a2down", f))
-    for r in range(H + 1):
+    def span_row(r):
         block_row(4, r, *conv_row(a2, (2, 3), w2p, r))
         block_row(5, r, *conv_row(a2, (3,), w2e, r))
-    for q in range(2):
-        for i, part in enumerate(shrink((4, 5), q)):
-            p_out[q, i] = part.astype(BF)
-    send("p", p_out, p_in, later)
-
-    take_a1(0)
+
+    def span_part(q):
+        for i, x in enumerate(shrink((4, 5), q)):
+            p_out[q, i] = x.astype(BF)
+        send("later", **{f"p{q}": (p_out.at[q], p_in.at[q])})
+
+    for r in (1, 2):
+        span_row(r)
+
+    arrived("a1down0", "a1up0", "s0", "s1")
     for r in (0, 3):
         second_act(1, r, *conv_row(a1, (0, 1, 2), w1f, r))
-    send_a2(1)
-
-    def first_frame(r):
-        even, odd = conv_row(a1, (0, 1), w1m, r)
-        se, so = halves(s_in[r].astype(F32))
+    send_a2(1, 1)
+    for r in (0, 3, 1, 2):
+        even, odd = conv_row(a1, (0, 1), w1m, r) if r in (0, 3) else (part[r - 1, 0], part[r - 1, 1])
+        se, so = halves(s_in[(2, 0, 1, 3)[r]].astype(F32))
         second_act(0, r, even + se, odd + so)
-
-    arrived("s")
-    for r in (0, 1, 3):
-        first_frame(r)
-    send_a2(0)
-    first_frame(2)
+    send_a2(0, 1)
+
+    arrived("a2down2", "a2up2")
+    span_row(0)
+    span_part(0)
+    for r in (3, 4):
+        span_row(r)
+    span_part(1)
 
     fetches["dg"].wait()
     fetches["ds"].wait()
@@ -292,9 +318,6 @@
             for p in range(H):
                 place[p] = jnp.where(jnp.logical_and(here, position == p), 2 * j + slot, place[p])
 
-    for f in range(H):
-        arrived(("vt", f))
-
     def block(f, r):
         frames, w = {3: ((1, 2, 3), w2f), 2: ((0, 1, 2), w2f), 1: ((0, 1), w2m), 0: ((0,), w2l)}[f]
         even, odd = conv_row(a2, frames, w, r)
@@ -313,41 +336,62 @@
             for slot in range(2):
                 sel[q, j, slot] = red[q, picks[2 * j + slot]]
         for j in (1, 0, 2):
-            send(("x", q, j), sel.at[q, j], got.at[q, pl.ds(2 * j, 2)], others[j])
+            send(j, **{f"x{q}{j}": (sel.at[q, j], got.at[q, pl.ds(2 * j, 2)])})
 
     for r in (1, 2):
         for f in (3, 2, 1, 0):
             block(f, r)
-    arrived(("a2down", 1))
-    arrived(("a2down", 0))
+    arrived("vt", "a2down1", "a2down0", "p0")
     for f in (3, 2, 1, 0):
         block(f, 0)
-    arrived("p")
     ship(0)
-    arrived(("a2up", 1))
-    arrived(("a2up", 0))
+    arrived("a2up1", "a2up0", "p1")
     for r in (3, 4):
         for f in (3, 2, 1, 0):
             block(f, r)
     ship(1)
 
-    fetches["prow"].wait()
-    pcol[...] = column(prow[...])
-    fetches["p"].wait()
     for q in range(2):
         for j in range(n_clips - 1):
-            arrived(("x", q, j))
-    bias = jnp.concatenate([pcol[...], pcol[...]], axis=1)
+            arrived(f"x{q}{j}")
     for p in range(H):
-        i = jnp.maximum(place[p], 0)
-        y = dot(pw[...], jnp.concatenate([got[0, i], got[1, i]], axis=1)) + bias
-        y = jnp.where(place[p] >= 0, y, 0.0)
-        out[p] = y.reshape(C2, 2, HALF).astype(BF)
-    for copy, sends, _ in copies.values():
-        under(sends, copy.wait_send)
-
-
-N_COPIES, N_FETCHES = 31, 16
+        for q in range(2):
+            x = got[q, jnp.maximum(place[p], 0)]
+            out[p, q] = jnp.where(place[p] >= 0, x, jnp.zeros_like(x))
+    each_way(copies, 2, lambda copy: copy.wait_send())
+
+
+def project(n_clips, dgh, dsh, xh, ph, bh, out, dg, ds, x, pw, row, y, sem, osem):
+    g = lax.axis_index("clips")
+    t = lax.axis_index("tm")
+    fetches = [
+        pltpu.make_async_copy(src, dst, sem.at[i])
+        for i, (src, dst) in enumerate(((dgh, dg), (dsh, ds), (xh, x), (ph, pw), (bh, row)))
+    ]
+    for copy in fetches:
+        copy.start()
+    for copy in fetches:
+        copy.wait()
+    bias = column(row[...])
+    bias = jnp.concatenate([bias, bias], axis=1)
+    stores = []
+    for p in range(H):
+        filled = jnp.int32(0)
+        for group in range(n_clips):
+            for f in range(H):
+                here = jnp.logical_and(dg[group, t * H + f] == g, ds[group, t * H + f] == p)
+                filled = jnp.where(here, 1, filled)
+        z = dot(pw[...], jnp.concatenate([x[p, 0], x[p, 1]], axis=1)) + bias
+        z = jnp.where(filled > 0, z, 0.0)
+        y[p] = z.reshape(C2, 2, HALF).astype(BF)
+        copy = pltpu.make_async_copy(y.at[p], out.at[p], osem.at[p])
+        copy.start()
+        stores.append(copy)
+    for copy in stores:
+        copy.wait()
+
+
+N_COPIES, N_FETCHES = 24, 14
 
 
 def local(
@@ -358,10 +402,10 @@
     hbm = pl.BlockSpec(memory_space=pltpu.HBM)
     row = lambda v: v.reshape(1, C)
     taps = 9 * C
-    packed = pl.pallas_call(
+    reduced = pl.pallas_call(
         functools.partial(kernel, sizes),
-        out_shape=jax.ShapeDtypeStruct((H, C2, 2, HALF), BF),
-        in_specs=[hbm] * 13,
+        out_shape=jax.ShapeDtypeStruct((H, 2, C, HALF), BF),
+        in_specs=[hbm] * 11,
         out_specs=vm,
         scratch_shapes=[
             pltpu.VMEM((H, C, H, W), BF),
@@ -373,6 +417,7 @@
             pltpu.VMEM((H, H + 3, C, W), BF),
             pltpu.VMEM((H, C, W), BF),
             pltpu.VMEM((H, C, W), BF),
+            pltpu.VMEM((2, 2, C, HALF), F32),
             pltpu.VMEM((H + 2, H + 1, 3, C, HALF), BF),
             pltpu.VMEM((2, H, C, HALF), BF),
             pltpu.VMEM((2, 2, C, HALF), BF),
@@ -382,7 +427,6 @@
             pltpu.VMEM((9, 3 * C, C), BF),
             pltpu.VMEM((9, 3 * C, C), BF),
             pltpu.VMEM((9, C, C), BF),
-            pltpu.VMEM((C2, C), BF),
             pltpu.VMEM((3 * C, taps), BF),
             pltpu.VMEM((3 * C, 6 * C), BF),
             pltpu.VMEM((3 * C, 3 * C), BF),
@@ -394,9 +438,7 @@
             pltpu.VMEM((C, taps), BF),
             pltpu.VMEM((W, W), BF),
             pltpu.VMEM((5, 1, C), F32),
-            pltpu.VMEM((1, C2), F32),
             pltpu.VMEM((5, C, HALF), F32),
-            pltpu.VMEM((C2, HALF), F32),
             pltpu.SMEM((4, 32), jnp.int32),
             pltpu.SMEM((4, 32), jnp.int32),
             pltpu.SemaphoreType.DMA((N_FETCHES,)),
@@ -410,10 +452,29 @@
         name="encode",
     )(
         dest_group, dest_slot, video[0], row(norm1_gain), row(conv1_bias), row(norm2_gain),
-        row(conv2_bias), row(down_bias), proj_bias.reshape(1, C2),
+        row(conv2_bias), row(down_bias),
         conv1_weight.reshape(9, 3 * C, C), conv2_weight.reshape(9, 3 * C, C),
-        down_weight.reshape(9, C, C), proj_weight,
+        down_weight.reshape(9, C, C),
     )
+    packed = pl.pallas_call(
+        functools.partial(project, sizes[0]),
+        out_shape=jax.ShapeDtypeStruct((H, C2, 2, HALF), BF),
+        in_specs=[hbm] * 5,
+        out_specs=hbm,
+        scratch_shapes=[
+            pltpu.SMEM((4, 32), jnp.int32),
+            pltpu.SMEM((4, 32), jnp.int32),
+            pltpu.VMEM((H, 2, C, HALF), BF),
+            pltpu.VMEM((C2, C), BF),
+            pltpu.VMEM((1, C2), F32),
+            pltpu.VMEM((H, C2, 2, HALF), BF),
+            pltpu.SemaphoreType.DMA((5,)),
+            pltpu.SemaphoreType.DMA((H,)),
+        ],
+        compiler_params=pltpu.CompilerParams(vmem_limit_bytes=63 << 20),
+        cost_estimate=pl.CostEstimate(flops=4 * 10**7, bytes_accessed=1 << 20, transcendentals=0),
+        name="project",
+    )(dest_group, dest_slot, reduced, proj_weight, proj_bias.reshape(1, C2))
     return packed[None, None]
 
 

time: 34.5 us -> 32.2 us (0.933)
  local copies, waits for them, and re-layouts: 2.01 us -> 0 us
    pallas_call x1, Pallas kernels: 32.3 us -> 29.7 us  [local(): pl.pallas_call(functools.partial(kernel, sizes), out_shape=jax.ShapeDtype...]
    pallas_call x0 -> x1, Pallas kernels: none -> 2.26 us  [local(): pl.pallas_call(functools.partial(project, sizes[0]), out_shape=jax.ShapeD...]
    unnamed x1 -> x0, local copies, waits for them, and re-layouts: 2.01 us -> none
where the time goes in v2:
time: 32.2 us; the launch traced here: 32 us
  Pallas kernels  32 us (99%)
    pallas_call x1, Pallas kernels, local(): pl.pallas_call(functools.partial(kernel, sizes), out_shape=jax.ShapeDtype...  29.7 us
    pallas_call x1, Pallas kernels, local(): pl.pallas_call(functools.partial(project, sizes[0]), out_shape=jax.ShapeD...  2.26 us

profile of v2, /device:TPU:217, one launch (start us, length us, event | category | flops | bytes accessed | tf_op | source)
XLA Modules:
  0.0 32.0 jit_solution(12040647525436510815)
XLA Ops:
  0.0 29.7 %encode.1.xh = bf16[4,2,96,128]{3,2,1,0:T(8,128)(2,1)} custom-call(s32[4,32]{1,0:T(4,128)} %dgh.3, s32[4,32]{1,0:T(4,128)} %dsh.3, bf16[4,96,4,256]{3,2,1,0:T(4,128)(2,1)} %bitcast.12, f32[1,96]{1,0:T(1,128)} %bitcast.16, f32[1,96]{1,0:T(1,128)} %bitcast.17, f32[1,96]{1,0:T(1,128)} %bitcast.18, f32[1,96]{1,0:T(1,128)} %bitcast.19, f32[1,96]{1,0:T(1,128)} %bitcast.20, ...), custom_call_target="tpu_custom_call" | custom-call | flops 5000000000 | bytes 3145728 | tf_op jit(solution)/shard_map/encode/pallas_call | solution.py:405
  29.7 2.3 %project.1 = bf16[4,192,2,128]{3,2,1,0:T(2,128)(2,1)} custom-call(s32[4,32]{1,0:T(4,128)} %dgh.3, s32[4,32]{1,0:T(4,128)} %dsh.3, bf16[4,2,96,128]{3,2,1,0:T(8,128)(2,1)} %encode.1.xh, bf16[192,96]{1,0:T(8,128)(2,1)} %ph.1, f32[1,192]{1,0:T(1,128)} %bitcast.11), custom_call_target="tpu_custom_call" | custom-call | flops 40000000 | bytes 1048576 | tf_op jit(solution)/shard_map/project/pallas_call | solution.py:459

commit v3 on v2

--- a/solution.py
+++ b/solution.py
@@ -26,11 +26,11 @@
 
 def kernel(
     sizes,
-    dgh, dsh, video, g1h, b1h, g2h, b2h, bdh, w1h, w2h, dh,
-    out,
-    vraw, vh, vht, vt, vn, a1, a2, s_out, s_in, part, bl, red, p_out, p_in, sel, got,
+    dgh, video, g1h, b1h, g2h, b2h, bdh, w1h, w2h, dh,
+    got,
+    vraw, vh, vht, vt, vn, a1, a2, s_out, s_in, part, bl, red, p_out, p_in, sel,
     w1raw, w2raw, draw, w1f, w1m, w1e, w2f, w2m, w2l, w2e, w2p, dw,
-    perm, rows, cols, dg, ds, lsem, ssem, rsem,
+    perm, rows, cols, dg, lsem, ssem, rsem,
 ):
     n_clips, n_tm, n_tile = sizes
     g = lax.axis_index("clips")
@@ -107,7 +107,6 @@
     fetch("w2", w2h, w2raw)
     fetch("d", dh, draw)
     fetch("dg", dgh, dg)
-    fetch("ds", dsh, ds)
 
     @pl.when(top)
     def _():
@@ -141,10 +140,8 @@
     )
     send("later", v=(video.at[3], vh))
 
-    for i in range(5):
-        fetches[("row", i)].wait()
-    for i in range(5):
-        cols[i] = column(rows[i])
+    fetches[("row", 0)].wait()
+    cols[0] = column(rows[0])
 
     lane = lax.broadcasted_iota(jnp.int32, (C, HALF), 1)
 
@@ -204,6 +201,12 @@
         return jnp.concatenate([raw[3 * i + j] for i in taps for j in range(3)], axis=1)
 
     fetches["w1"].wait()
+    fetches["w2"].wait()
+    fetches["d"].wait()
+    for i in range(1, 5):
+        fetches[("row", i)].wait()
+    for i in range(1, 5):
+        cols[i] = column(rows[i])
     w1e[...] = gather_taps(w1raw, (0,))
     w1f[...] = gather_taps(w1raw, (0, 1, 2))
     w1m[...] = gather_taps(w1raw, (1, 2))
@@ -219,29 +222,28 @@
     for r in (1, 2):
         second_act(3, r, *conv_row(a1, (2, 3, 4), w1f, r))
         second_act(2, r, *conv_row(a1, (1, 2, 3), w1f, r))
-    send("later", s0=(s_out.at[pl.ds(0, 2)], s_in.at[pl.ds(0, 2)]))
-    fetches["w2"].wait()
-    fetches["d"].wait()
     w2f[...] = gather_taps(w2raw, (0, 1, 2))
     w2p[...] = gather_taps(w2raw, (0, 1))
     w2m[...] = gather_taps(w2raw, (1, 2))
     w2e[...] = gather_taps(w2raw, (0,))
     w2l[...] = gather_taps(w2raw, (2,))
     dw[...] = jnp.concatenate([draw[i] for i in range(9)], axis=1)
+    send("later", s0=(s_out.at[pl.ds(0, 2)], s_in.at[pl.ds(0, 2)]))
 
     arrived("a1down3", "a1up3", "a1down1", "a1up1")
     for r in (0, 3):
         early_tap(r)
-    for r in (0, 3):
-        second_act(3, r, *conv_row(a1, (2, 3, 4), w1f, r))
-        second_act(2, r, *conv_row(a1, (1, 2, 3), w1f, r))
     send("later", s1=(s_out.at[pl.ds(2, 2)], s_in.at[pl.ds(2, 2)]))
-    send_a2(2, 2)
 
     arrived("v")
     turn(vh[...], vht)
     first_act(vht, 0)
     send_a1(0, 1)
+
+    for r in (0, 3):
+        second_act(3, r, *conv_row(a1, (2, 3, 4), w1f, r))
+        second_act(2, r, *conv_row(a1, (1, 2, 3), w1f, r))
+    send_a2(2, 2)
 
     for r in (1, 2):
         second_act(1, r, *conv_row(a1, (0, 1, 2), w1f, r))
@@ -290,7 +292,6 @@
     span_part(1)
 
     fetches["dg"].wait()
-    fetches["ds"].wait()
 
     def target(group, f):
         return dg[group, t * H + f]
@@ -307,16 +308,6 @@
             for f, (to, order) in enumerate(own):
                 frame = jnp.where(jnp.logical_and(to == group, order == slot), f, frame)
             picks.append(frame)
-    place = [jnp.int32(-1)] * H
-    for j in range(n_clips):
-        mine = j == n_clips - 1
-        group = g if mine else lax.rem(g + n_clips - 1 - j, n_clips)
-        for f in range(H):
-            slot = jnp.int32(f) if mine else rank(group, f)
-            here = target(group, f) == g
-            position = ds[group, t * H + f]
-            for p in range(H):
-                place[p] = jnp.where(jnp.logical_and(here, position == p), 2 * j + slot, place[p])
 
     def block(f, r):
         frames, w = {3: ((1, 2, 3), w2f), 2: ((0, 1, 2), w2f), 1: ((0, 1), w2m), 0: ((0,), w2l)}[f]
@@ -331,7 +322,7 @@
                     part = part + p_in[q, f].astype(F32)
                 part = (part + cols[4]).astype(BF)
                 red[q, f] = part
-                got[q, 6 + f] = part
+        fetch(("own", q), red.at[q], got.at[q, pl.ds(6, H)])
         for j in range(n_clips - 1):
             for slot in range(2):
                 sel[q, j, slot] = red[q, picks[2 * j + slot]]
@@ -341,23 +332,23 @@
     for r in (1, 2):
         for f in (3, 2, 1, 0):
             block(f, r)
-    arrived("vt", "a2down1", "a2down0", "p0")
+    arrived("vt", "a2down1", "a2down0")
     for f in (3, 2, 1, 0):
         block(f, 0)
+    arrived("p0")
     ship(0)
-    arrived("a2up1", "a2up0", "p1")
+    arrived("a2up1", "a2up0")
     for r in (3, 4):
         for f in (3, 2, 1, 0):
             block(f, r)
+    arrived("p1")
     ship(1)
 
     for q in range(2):
         for j in range(n_clips - 1):
             arrived(f"x{q}{j}")
-    for p in range(H):
-        for q in range(2):
-            x = got[q, jnp.maximum(place[p], 0)]
-            out[p, q] = jnp.where(place[p] >= 0, x, jnp.zeros_like(x))
+    for q in range(2):
+        fetches[("own", q)].wait()
     each_way(copies, 2, lambda copy: copy.wait_send())
 
 
@@ -370,19 +361,34 @@
     ]
     for copy in fetches:
         copy.start()
-    for copy in fetches:
-        copy.wait()
+    fetches[4].wait()
     bias = column(row[...])
     bias = jnp.concatenate([bias, bias], axis=1)
+    fetches[0].wait()
+    fetches[1].wait()
+
+    def target(group, f):
+        return dg[group, t * H + f]
+
+    place = [jnp.int32(-1)] * H
+    for j in range(n_clips):
+        mine = j == n_clips - 1
+        group = g if mine else lax.rem(g + n_clips - 1 - j, n_clips)
+        slot = jnp.int32(0)
+        for f in range(H):
+            here = target(group, f) == g
+            position = ds[group, t * H + f]
+            source = jnp.int32(6 + f) if mine else 2 * j + slot
+            for p in range(H):
+                place[p] = jnp.where(jnp.logical_and(here, position == p), source, place[p])
+            slot = slot + jnp.int32(here)
+    fetches[3].wait()
+    fetches[2].wait()
     stores = []
     for p in range(H):
-        filled = jnp.int32(0)
-        for group in range(n_clips):
-            for f in range(H):
-                here = jnp.logical_and(dg[group, t * H + f] == g, ds[group, t * H + f] == p)
-                filled = jnp.where(here, 1, filled)
-        z = dot(pw[...], jnp.concatenate([x[p, 0], x[p, 1]], axis=1)) + bias
-        z = jnp.where(filled > 0, z, 0.0)
+        i = jnp.maximum(place[p], 0)
+        z = dot(pw[...], jnp.concatenate([x[0, i], x[1, i]], axis=1)) + bias
+        z = jnp.where(place[p] >= 0, z, 0.0)
         y[p] = z.reshape(C2, 2, HALF).astype(BF)
         copy = pltpu.make_async_copy(y.at[p], out.at[p], osem.at[p])
         copy.start()
@@ -391,22 +397,21 @@
         copy.wait()
 
 
-N_COPIES, N_FETCHES = 24, 14
+N_COPIES, N_FETCHES = 24, 15
 
 
 def local(
     video, norm1_gain, conv1_weight, conv1_bias, norm2_gain, conv2_weight, conv2_bias,
     down_weight, down_bias, proj_weight, proj_bias, dest_group, dest_slot, sizes,
 ):
-    vm = pl.BlockSpec(memory_space=pltpu.VMEM)
     hbm = pl.BlockSpec(memory_space=pltpu.HBM)
     row = lambda v: v.reshape(1, C)
     taps = 9 * C
     reduced = pl.pallas_call(
         functools.partial(kernel, sizes),
-        out_shape=jax.ShapeDtypeStruct((H, 2, C, HALF), BF),
-        in_specs=[hbm] * 11,
-        out_specs=vm,
+        out_shape=jax.ShapeDtypeStruct((2, 10, C, HALF), BF),
+        in_specs=[hbm] * 10,
+        out_specs=hbm,
         scratch_shapes=[
             pltpu.VMEM((H, C, H, W), BF),
             pltpu.VMEM((C, H, W), BF),
@@ -423,7 +428,6 @@
             pltpu.VMEM((2, 2, C, HALF), BF),
             pltpu.VMEM((2, 2, C, HALF), BF),
             pltpu.VMEM((2, 3, 2, C, HALF), BF),
-            pltpu.VMEM((2, 10, C, HALF), BF),
             pltpu.VMEM((9, 3 * C, C), BF),
             pltpu.VMEM((9, 3 * C, C), BF),
             pltpu.VMEM((9, C, C), BF),
@@ -440,7 +444,6 @@
             pltpu.VMEM((5, 1, C), F32),
             pltpu.VMEM((5, C, HALF), F32),
             pltpu.SMEM((4, 32), jnp.int32),
-            pltpu.SMEM((4, 32), jnp.int32),
             pltpu.SemaphoreType.DMA((N_FETCHES,)),
             pltpu.SemaphoreType.DMA((N_COPIES,)),
             pltpu.SemaphoreType.DMA((N_COPIES,)),
@@ -451,7 +454,7 @@
         cost_estimate=pl.CostEstimate(flops=5 * 10**9, bytes_accessed=3 << 20, transcendentals=1 << 20),
         name="encode",
     )(
-        dest_group, dest_slot, video[0], row(norm1_gain), row(conv1_bias), row(norm2_gain),
+        dest_group, video[0], row(norm1_gain), row(conv1_bias), row(norm2_gain),
         row(conv2_bias), row(down_bias),
         conv1_weight.reshape(9, 3 * C, C), conv2_weight.reshape(9, 3 * C, C),
         down_weight.reshape(9, C, C),
@@ -464,7 +467,7 @@
         scratch_shapes=[
             pltpu.SMEM((4, 32), jnp.int32),
             pltpu.SMEM((4, 32), jnp.int32),
-            pltpu.VMEM((H, 2, C, HALF), BF),
+            pltpu.VMEM((2, 10, C, HALF), BF),
             pltpu.VMEM((C2, C), BF),
             pltpu.VMEM((1, C2), F32),
             pltpu.VMEM((H, C2, 2, HALF), BF),

time: 32.2 us -> 31.8 us (0.988)
  the two profiles are of different devices: /device:TPU:217 before, /device:TPU:225 now
where the time goes in v3:
time: 31.8 us; the launch traced here: 31.7 us
  Pallas kernels  31.7 us (100%)
    pallas_call x1, Pallas kernels, local(): pl.pallas_call(functools.partial(kernel, sizes), out_shape=jax.ShapeDtype...  29.3 us
    pallas_call x1, Pallas kernels, local(): pl.pallas_call(functools.partial(project, sizes[0]), out_shape=jax.ShapeD...  2.4 us

profile of v3, /device:TPU:225, one launch (start us, length us, event | category | flops | bytes accessed | tf_op | source)
XLA Modules:
  0.0 31.7 jit_solution(3529463891994516944)
XLA Ops:
  0.0 29.3 %encode.1.xh = bf16[2,10,96,128]{3,2,1,0:T(8,128)(2,1)} custom-call(s32[4,32]{1,0:T(4,128)} %dgh.3, bf16[4,96,4,256]{3,2,1,0:T(4,128)(2,1)} %bitcast.12, f32[1,96]{1,0:T(1,128)} %bitcast.16, f32[1,96]{1,0:T(1,128)} %bitcast.17, f32[1,96]{1,0:T(1,128)} %bitcast.18, f32[1,96]{1,0:T(1,128)} %bitcast.19, f32[1,96]{1,0:T(1,128)} %bitcast.20, ...), custom_call_target="tpu_custom_call" | custom-call | flops 5000000000 | bytes 3145728 | tf_op jit(solution)/shard_map/encode/pallas_call | solution.py:410
  29.3 2.4 %project.1 = bf16[4,192,2,128]{3,2,1,0:T(2,128)(2,1)} custom-call(s32[4,32]{1,0:T(4,128)} %dgh.3, s32[4,32]{1,0:T(4,128)} %dsh.1, bf16[2,10,96,128]{3,2,1,0:T(8,128)(2,1)} %encode.1.xh, bf16[192,96]{1,0:T(8,128)(2,1)} %ph.1, f32[1,192]{1,0:T(1,128)} %bitcast.11), custom_call_target="tpu_custom_call" | custom-call | flops 40000000 | bytes 1048576 | tf_op jit(solution)/shard_map/project/pallas_call | solution.py:462
